TPU v7x, 32 devices: a whole 2x2x4 slice. The times are simulated.
32 devices in a mesh: dp: 8 (over y, x, core), ctx: 4 (over z).
Axes of the slice: x: 2, y: 2, z: 4, core: 2. Of those that a mesh axis runs over, the one named last changes fastest.
Arguments:
- queries: bfloat16 [8, 4096, 512], P('dp', 'ctx'), may hold values from -6 to 6
- keys: bfloat16 [8, 4096, 128], P('dp', 'ctx'), may hold values from -6 to 6
- values: bfloat16 [8, 4096, 128], P('dp', 'ctx'), may hold values from -6 to 6
- dest_replica: int32 [8, 64], P('dp', 'ctx'), may hold values from 0 to 7, as said below
- dest_slot: int32 [8, 64], P('dp', 'ctx'), may hold values from 0 to 63, as said below
- doc_lengths: int32 [8, 16], P('dp'), may hold values from 1 to 32, 64 in all within a row
- tile_mask: int32 [8, 64, 64], P('dp', 'ctx'), may hold values 0 or 1
Outputs:
- attended: bfloat16 [8, 4096, 512], P('dp', 'ctx')
Inputs may be any that keep to these rules, and one draw needn't show every extreme that they name: `dest_replica`: every block of a pack receives exactly one arriving block; a block keeps its shard along ctx (dest_slot // 16 equals the arriving block's own b // 16); the 16 blocks of one device go to every pack, 2 to each. `dest_slot`: see dest_replica. `doc_lengths`: they sum to 64 in every pack, and the largest is 32 in every pack.
All inputs are finite; a program needn't handle non-finite values. No bound on the sum of `tile_mask` on one device may be relied on, other than what follows from the above.
Results may differ from a plain program's by a relative error of at most 0.0033.
Values may be sent and summed in bfloat16 or wider, within the bound.
No kernel may reach another device: no remote copies, remote signals or barrier semaphores. Data moves between devices by JAX's collectives and lax.ppermute only.
A program may use at most 64 MiB of HBM per device.

v0:
```python
import functools

import jax
import jax.numpy as jnp
from jax import lax
from jax.experimental import pallas as pl
from jax.experimental.pallas import tpu as pltpu
from jax.sharding import PartitionSpec as P

HEAD_WIDTH = 128
QUERY_HEADS = 4
SCALE = HEAD_WIDTH ** (-0.5) * 1.4426950408889634
NEVER = -1e30
MOST = 1e30
CHUNK = 256
SLOT_ROWS = 16
REACH = 2
PIECE = 4
VMEM_LIMIT = 32 * 1024 * 1024
VMEM_SMALL = 8 * 1024 * 1024

ANY = pl.BlockSpec(memory_space=pl.ANY)
SMEM = pl.BlockSpec(memory_space=pltpu.SMEM)
VMEM = pl.BlockSpec(memory_space=pltpu.VMEM)


def shifted(value, axis):
    count = lax.axis_size(axis)
    return lax.ppermute(value, axis, [(source, source + 1) for source in range(count - 1)])


def pack_kv_kernel(cap, targets, slots, keys, values, send, counts, slot_of):
    packs = send.shape[0]
    blocks = targets.shape[1]
    size = keys.shape[1] // blocks
    half = cap * size
    for t in range(packs):
        counts[t] = 0
    for j in range(blocks):
        t = targets[0, j]
        rank = counts[t]
        counts[t] = rank + 1
        slot_of[t * cap + rank] = lax.rem(slots[0, j], blocks)
        rows = slice(j * size, (j + 1) * size)
        to = pl.multiple_of(rank * size, size)
        send[t, pl.ds(to, size), :] = keys[0, rows, :]
        send[t, pl.ds(to + half, size), :] = values[0, rows, :]
    row = lax.broadcasted_iota(jnp.int32, (SLOT_ROWS, HEAD_WIDTH), 0)
    for t in range(packs):
        listed = jnp.zeros(row.shape, jnp.int32)
        for i in range(cap):
            listed = jnp.where(row == i, slot_of[t * cap + i], listed)
        send[t, 2 * half:, :] = listed.astype(jnp.float32).astype(jnp.bfloat16)


def pack_q_kernel(cap, targets, lengths, tiles, queries, send, bias, block_of, counts):
    packs = send.shape[0]
    blocks = targets.shape[1]
    tokens = queries.shape[1]
    size = tokens // blocks
    place = lax.axis_index("ctx")
    for t in range(packs):
        counts[t] = 0
    for j in range(blocks):
        t = targets[0, j]
        rank = counts[t]
        counts[t] = rank + 1
        to = pl.multiple_of(rank * size, size)
        send[t, pl.ds(to, size), :] = queries[0, j * size:(j + 1) * size, :]

    block = lax.broadcasted_iota(jnp.int32, (tokens, HEAD_WIDTH), 1)
    of_key = lax.broadcasted_iota(jnp.int32, (tokens, HEAD_WIDTH), 0) // size
    block_of[...] = (block == of_key).astype(jnp.float32).astype(jnp.bfloat16)
    query_block = place * blocks + lax.broadcasted_iota(jnp.int32, (blocks, 1), 0)
    listed_tiles = tiles[0].astype(jnp.float32).astype(jnp.bfloat16)
    for offset in range(bias.shape[0]):
        low = (place - offset) * blocks
        key_block = low + lax.broadcasted_iota(jnp.int32, (1, HEAD_WIDTH), 1)
        key_doc = jnp.zeros((1, HEAD_WIDTH), jnp.int32)
        query_doc = jnp.zeros((blocks, 1), jnp.int32)
        end = jnp.int32(0)
        for j in range(lengths.shape[1]):
            end = end + lengths[0, j]
            key_doc = key_doc + (key_block >= end).astype(jnp.int32)
            query_doc = query_doc + (query_block >= end).astype(jnp.int32)
        spread = lax.broadcasted_iota(jnp.int32, (tiles.shape[2], HEAD_WIDTH), 0) == key_block
        listed = jnp.dot(
            listed_tiles, spread.astype(jnp.float32).astype(jnp.bfloat16),
            preferred_element_type=jnp.float32,
        )
        allowed = (query_doc == key_doc) & (key_block <= query_block) & (key_block >= 0)
        allowed = allowed & ((listed > 0.5) | (key_block == query_block))
        bias[offset] = jnp.where(allowed, 0.0, NEVER)


def place_kernel(cap, received, early, rest, order, placed):
    packs = received.shape[0]
    tokens = placed.shape[0] // 2
    size = tokens // (packs * cap)
    half = cap * size
    for s in range(packs):
        listed = received[s, 2 * half:, :].astype(jnp.float32).astype(jnp.int32)
        for i in range(cap):
            slot = listed[i, 0]
            order[0, slot] = s * cap + i
            to = pl.multiple_of(slot * size, size)
            placed[pl.ds(to, size), :] = received[s, i * size:(i + 1) * size, :]
            placed[pl.ds(to + tokens, size), :] = (
                received[s, half + i * size:half + (i + 1) * size, :]
            )
    early[...] = placed[:early.shape[0], :]
    rest[...] = placed[early.shape[0]:, :]


def first_document(lengths, position):
    start, end = jnp.int32(0), jnp.int32(0)
    total = jnp.int32(0)
    for j in range(lengths.shape[1]):
        after = total + lengths[0, j]
        inside = (total <= position) & (position < after)
        start = jnp.where(inside, total, start)
        end = jnp.where(inside, after, end)
        total = after
    return start, end


def reach_of(lengths, place, offset, blocks):
    start, end = first_document(lengths, place * blocks)
    low = (place - offset) * blocks
    rows = jnp.where(start < low + blocks, jnp.minimum(end - place * blocks, blocks), 0)
    return jnp.where(low >= 0, rows, 0), jnp.maximum(start - low, 0)


def keys_of(early, rest, low, high):
    half = early.shape[0]
    if high <= half:
        return early[low:high, :]
    if low >= half:
        return rest[low - half:high - half, :]
    return jnp.concatenate([early[low:, :], rest[:high - half, :]], axis=0)


def values_of(early, rest, low, high):
    values = (early.shape[0] + rest.shape[0]) // 2 - early.shape[0]
    return beside_ones(rest[values + low:values + high, :])


def beside_ones(values):
    return jnp.concatenate([values, jnp.ones(values.shape, values.dtype)], axis=1)


def query_rows(received, order, bias, i, size):
    source = pl.ds(pl.multiple_of(order[0, i] * size, size), size)
    barred = jnp.broadcast_to(bias[pl.ds(i, 1), :], (QUERY_HEADS * size, HEAD_WIDTH))
    return jnp.concatenate(
        [heads_as_rows(received[source, :]), barred.astype(jnp.bfloat16)], axis=1
    )


def pair_rows(received, order, bias, i, size):
    return jnp.concatenate(
        [query_rows(received, order, bias, i + u, size) for u in range(2)], axis=0
    )


def score(rows, keys, block_of):
    return lax.dot_general(
        rows, jnp.concatenate([keys, block_of], axis=1), (((1,), (1,)), ((), ())),
        preferred_element_type=jnp.float32,
    )


def weigh(scores, level):
    return jnp.exp2(scores * SCALE - level).astype(jnp.bfloat16)


def largest(sums, so_far):
    parts = sums[:, HEAD_WIDTH:]
    return jnp.maximum(so_far, jnp.max(parts.reshape(-1, 8, HEAD_WIDTH), axis=0))


def divided(sums, size):
    ratio = sums[:, :HEAD_WIDTH] / sums[:, HEAD_WIDTH:]
    group = QUERY_HEADS * size
    return jnp.concatenate(
        [heads_as_columns(ratio[u:u + group], size) for u in range(0, ratio.shape[0], group)],
        axis=0,
    ).astype(jnp.bfloat16)


def heads_as_rows(block):
    return jnp.concatenate(
        [block[:, h * HEAD_WIDTH:(h + 1) * HEAD_WIDTH] for h in range(QUERY_HEADS)], axis=0
    )


def heads_as_columns(rows, size):
    return jnp.concatenate(
        [rows[h * size:(h + 1) * size] for h in range(QUERY_HEADS)], axis=1
    )


def own_kernel(
    order, bias_in, block_of, received, early, rest,
    out, state, level,
    stage, sem,
):
    bias = bias_in.at[0]
    blocks = bias.shape[0]
    tokens = (early.shape[0] + rest.shape[0]) // 2
    size = tokens // blocks
    group = QUERY_HEADS * size
    row = lax.broadcasted_iota(jnp.int32, (2 * group, 2 * size), 0)
    lane = lax.broadcasted_iota(jnp.int32, (2 * group, 2 * size), 1)
    later = lane - (row // group) * size > lax.rem(row, size)

    work = []
    for i in range(0, blocks, 2):
        width = (i + 2) * size
        spans = [(low, min(low + CHUNK, width)) for low in range(0, width, CHUNK)]
        for n, span in enumerate(spans[-1:] + spans[:-1]):
            work.append((i, span, n == 0, n == len(spans) - 1))

    rows = {}

    def start(i, span):
        if i not in rows:
            rows[i] = pair_rows(received, order, bias, i, size)
        return score(rows[i], keys_of(early, rest, *span), block_of[span[0]:span[1], :])

    worst = jnp.zeros((8, HEAD_WIDTH), jnp.float32)
    copies = []
    scores = start(*work[0][:2])
    for n, (i, span, opening, closing) in enumerate(work):
        ahead = start(*work[n + 1][:2]) if n + 1 < len(work) else None
        if opening:
            cut = span[1] - span[0] - 2 * size
            tail = jnp.where(later, NEVER, scores[:, cut:])
            scores = jnp.concatenate([scores[:, :cut], tail], axis=1) if cut else tail
            top = jnp.max(scores, axis=1, keepdims=True) * SCALE
            weights = []
            width = span[1]
        weights.append(weigh(scores, top))
        if closing:
            ordered = weights[1:] + weights[:1]
            joined = jnp.concatenate(ordered, axis=1) if len(ordered) > 1 else ordered[0]
            sums = jnp.dot(
                joined, values_of(early, rest, 0, width), preferred_element_type=jnp.float32
            )
            worst = largest(sums, worst)
            where = slice(i * group, (i + 2) * group)
            held = slice(i * size, (i + 2) * size)
            state[where, :] = sums
            level[where, :] = jnp.broadcast_to(top, (2 * group, HEAD_WIDTH))
            stage[held, :] = divided(sums, size)
            copy = pltpu.make_async_copy(stage.at[held], out.at[0, held], sem.at[i])
            copy.start()
            copies.append(copy)
        scores = ahead
    for copy in copies:
        copy.wait()

    @pl.when(jnp.logical_not(jnp.max(worst) < MOST))
    def _():
        def again(i, carry):
            where = pl.ds(pl.multiple_of(i * group, group), group)
            held = pl.ds(pl.multiple_of(i * size, size), size)
            scores = score(
                query_rows(received, order, bias, i, size),
                keys_of(early, rest, 0, tokens), block_of[...],
            )
            query = i * size + lax.rem(lax.broadcasted_iota(jnp.int32, scores.shape, 0), size)
            key = lax.broadcasted_iota(jnp.int32, scores.shape, 1)
            scores = jnp.where(key > query, NEVER, scores)
            top = jnp.max(scores, axis=1, keepdims=True) * SCALE
            sums = jnp.dot(
                weigh(scores, top), values_of(early, rest, 0, tokens),
                preferred_element_type=jnp.float32,
            )
            state[where, :] = sums
            level[where, :] = jnp.broadcast_to(top, (group, HEAD_WIDTH))
            stage[held, :] = divided(sums, size)
            copy = pltpu.make_async_copy(stage.at[held], out.at[0, held], sem.at[0])
            copy.start()
            copy.wait()
            return carry

        lax.fori_loop(0, blocks, again, 0)


def hop_kernel(
    offset, order, lengths, bias_in, block_of, received, early, rest,
    out_in, level_in, state_in, *refs,
):
    stage, sem = refs[-2:]
    out, level = refs[0], refs[1]
    place = lax.axis_index("ctx")
    bias = bias_in.at[offset]
    blocks = bias.shape[0]
    tokens = (early.shape[0] + rest.shape[0]) // 2
    size = tokens // blocks
    group = QUERY_HEADS * size
    reads, first = reach_of(lengths, place, offset, blocks)

    def over(low, together, final):
        def keep(i, sums):
            count = sums.shape[0]
            if offset < REACH:
                refs[2][pl.ds(pl.multiple_of(i * group, group), count), :] = sums
            if final:
                held = pl.ds(pl.multiple_of(i * size, size), count // QUERY_HEADS)
                stage[held, :] = divided(sums, size)

        spans = [(at, at + CHUNK) for at in range(low, tokens, CHUNK)]
        work = [(u, span) for u in range(0, together, 2) for span in spans]

        def step(n, worst):
            i = n * together
            rows = {}

            def start(u, span):
                if u not in rows:
                    rows[u] = pair_rows(received, order, bias, i + u, size)
                return score(rows[u], keys_of(early, rest, *span), block_of[span[0]:span[1], :])

            scores = start(*work[0])
            for m, (u, span) in enumerate(work):
                ahead = start(*work[m + 1]) if m + 1 < len(work) else None
                where = pl.ds(pl.multiple_of((i + u) * group, group), 2 * group)
                if span is spans[0]:
                    base = level_in[where, :]
                    base = jnp.concatenate([base] * (CHUNK // HEAD_WIDTH), axis=1)
                    weights = []
                weights.append(weigh(scores, base))
                if span is spans[-1]:
                    joined = jnp.concatenate(weights, axis=1) if len(weights) > 1 else weights[0]
                    sums = state_in[where, :] + jnp.dot(
                        joined, values_of(early, rest, low, tokens), preferred_element_type=jnp.float32
                    )
                    worst = jnp.where(i + u < reads, largest(sums, worst), worst)
                    keep(i + u, sums)
                scores = ahead
            if final:
                lax.fori_loop(i, jnp.minimum(i + together, reads), send, 0)
            return worst

        def copy_of(i):
            held = pl.ds(pl.multiple_of(i * size, size), size)
            return pltpu.make_async_copy(stage.at[held], out.at[0, held], sem)

        def send(i, carry):
            copy_of(i).start()
            return carry

        def finish(i, carry):
            copy_of(i).wait()
            return carry

        steps = pl.cdiv(reads, together)
        worst = lax.fori_loop(0, steps, step, jnp.zeros((8, HEAD_WIDTH), jnp.float32))
        if final:
            lax.fori_loop(0, reads, finish, 0)

        @pl.when(jnp.logical_not(jnp.max(worst) < MOST))
        def _():
            def again(i, carry):
                where = pl.ds(pl.multiple_of(i * group, group), group)
                scores = score(
                    query_rows(received, order, bias, i, size),
                    keys_of(early, rest, 0, tokens), block_of[...],
                )
                before = level_in[where, :]
                top = jnp.max(scores, axis=1, keepdims=True) * SCALE
                now = jnp.maximum(before, top)
                factor = jnp.exp2(before - now)
                sums = jnp.concatenate([factor, factor], axis=1) * state_in[where, :] + jnp.dot(
                    weigh(scores, now[:, :1]), values_of(early, rest, 0, tokens),
                    preferred_element_type=jnp.float32,
                )
                level[where, :] = now
                keep(i, sums)
                if final:
                    copy_of(i).start()
                    copy_of(i).wait()
                return carry

            lax.fori_loop(0, reads, again, 0)

    part = first // (blocks // 4)
    more = jnp.int32(0)
    if offset < REACH:
        more, _ = reach_of(lengths, place, offset + 1, blocks)
        pl.when((reads > 0) & (more > 0))(functools.partial(over, 0, 4, False))
    for n, together in enumerate((4, 4, 8, 8)):
        pl.when((reads > 0) & (more == 0) & (part == n))(
            functools.partial(over, n * (tokens // 4), together, True)
        )


def per_device(queries, keys, values, dest_replica, dest_slot, doc_lengths, tile_mask):
    tokens = queries.shape[1]
    width = queries.shape[2]
    blocks = dest_replica.shape[1]
    size = tokens // blocks
    packs = lax.axis_size("dp")
    cap = blocks // packs
    bf16, f32 = jnp.bfloat16, jnp.float32
    rows = tokens * QUERY_HEADS
    params = pltpu.CompilerParams(vmem_limit_bytes=VMEM_LIMIT)
    small = pltpu.CompilerParams(vmem_limit_bytes=VMEM_SMALL)

    def cost(flops, moved):
        return pl.CostEstimate(flops=flops, bytes_accessed=moved, transcendentals=0)

    def route(sent):
        return lax.all_to_all(sent, "dp", split_axis=0, concat_axis=0, tiled=True)

    dma = pltpu.SemaphoreType.DMA
    counts = pltpu.SMEM((packs,), jnp.int32)
    kv_send = pl.pallas_call(
        functools.partial(pack_kv_kernel, cap),
        out_shape=jax.ShapeDtypeStruct((packs, 2 * cap * size + SLOT_ROWS, HEAD_WIDTH), bf16),
        in_specs=[SMEM, SMEM, VMEM, VMEM],
        out_specs=VMEM,
        scratch_shapes=[counts, pltpu.SMEM((blocks,), jnp.int32)],
        cost_estimate=cost(0, 4 * tokens * HEAD_WIDTH * 2),
        name="pack_kv",
    )(dest_replica, dest_slot, keys, values)
    kv_recv = route(kv_send)
    q_send, bias, block_of = pl.pallas_call(
        functools.partial(pack_q_kernel, cap),
        out_shape=(
            jax.ShapeDtypeStruct((packs, cap * size, width), bf16),
            jax.ShapeDtypeStruct((REACH + 1, blocks, HEAD_WIDTH), f32),
            jax.ShapeDtypeStruct((tokens, HEAD_WIDTH), bf16),
        ),
        in_specs=[SMEM, SMEM, VMEM, VMEM],
        out_specs=(VMEM, VMEM, VMEM),
        scratch_shapes=[counts],
        compiler_params=small,
        cost_estimate=cost(0, 2 * tokens * width * 2),
        name="pack_q",
    )(dest_replica, doc_lengths, tile_mask, queries)
    q_recv = route(q_send).reshape(tokens, width)
    piece = tokens * PIECE // 4
    early, rest, order = pl.pallas_call(
        functools.partial(place_kernel, cap),
        out_shape=(
            jax.ShapeDtypeStruct((piece, HEAD_WIDTH), bf16),
            jax.ShapeDtypeStruct((2 * tokens - piece, HEAD_WIDTH), bf16),
            jax.ShapeDtypeStruct((1, blocks), jnp.int32),
        ),
        in_specs=[VMEM],
        out_specs=(VMEM, VMEM, SMEM),
        scratch_shapes=[pltpu.VMEM((2 * tokens, HEAD_WIDTH), bf16)],
        compiler_params=small,
        cost_estimate=cost(0, 4 * tokens * HEAD_WIDTH * 2),
        name="place_kv",
    )(kv_recv)

    out_shape = jax.ShapeDtypeStruct((1, tokens, width), bf16)
    level_shape = jax.ShapeDtypeStruct((rows, HEAD_WIDTH), f32)
    sums_shape = jax.ShapeDtypeStruct((rows, 2 * HEAD_WIDTH), f32)
    stage = pltpu.VMEM((tokens, width), bf16)

    def attend_back(offset, early, rest, out, level, sums):
        last = offset == REACH
        return pl.pallas_call(
            functools.partial(hop_kernel, offset),
            out_shape=(out_shape, level_shape) + (() if last else (sums_shape,)),
            in_specs=[SMEM, SMEM] + [VMEM] * 5 + [ANY, VMEM, VMEM],
            out_specs=(ANY, VMEM) + (() if last else (VMEM,)),
            scratch_shapes=[stage, dma],
            input_output_aliases={7: 0, 8: 1},
            compiler_params=params,
            cost_estimate=cost(2 * 2 * rows * tokens * HEAD_WIDTH, 8 * tokens * width),
            name=f"attend_back_{offset}",
        )(order, doc_lengths, bias, block_of, q_recv, early, rest, out, level, sums)

    back_early = shifted(early, "ctx")
    back_rest = shifted(rest, "ctx")
    out, sums, level = pl.pallas_call(
        own_kernel,
        out_shape=(out_shape, sums_shape, level_shape),
        in_specs=[SMEM] + [VMEM] * 5,
        out_specs=(ANY, VMEM, VMEM),
        scratch_shapes=[stage, dma((blocks,))],
        compiler_params=params,
        cost_estimate=cost(2 * rows * tokens * HEAD_WIDTH, 8 * tokens * width),
        name="attend_own",
    )(order, bias, block_of, q_recv, early, rest)
    far_rest, out, sums, level = lax.optimization_barrier((back_rest, out, sums, level))
    far_early = shifted(back_early, "ctx")
    far_rest = shifted(far_rest, "ctx")
    out, level, sums = attend_back(1, back_early, back_rest, out, level, sums)
    return attend_back(2, far_early, far_rest, out, level, sums)[0]


def solution(mesh):
    return jax.shard_map(
        per_device,
        mesh=mesh,
        in_specs=(
            P("dp", "ctx", None),
            P("dp", "ctx", None),
            P("dp", "ctx", None),
            P("dp", "ctx"),
            P("dp", "ctx"),
            P("dp", None),
            P("dp", "ctx", None),
        ),
        out_specs=P("dp", "ctx", None),
        check_vma=False,
    )
```

profile of v0, /device:TPU:30, one launch (start us, length us, event | category | flops | bytes accessed | tf_op | source)
XLA Modules:
  0.0 52.0 jit_solution(6926394145082319529)
XLA Ops:
  0.0 0.0 copy-start.3
  0.0 0.0 copy-start.2
  0.0 0.0 copy-start.1
  0.0 0.0 copy-start
  0.0 2.1 %pack_kv.1 = bf16[8,272,128]{2,1,0:T(8,128)(2,1)} custom-call(s32[1,16]{1,0:T(1,128)} %targets.3, s32[1,16]{1,0:T(1,128)} %slots.1, bf16[1,1024,128]{2,1,0:T(8,128)(2,1)} %keys.1, bf16[1,1024,128]{2,1,0:T(8,128)(2,1)} %values.1), custom_call_target="tpu_custom_call" | custom-call | bytes 1048576 | tf_op jit(solution)/shard_map/pack_kv/pallas_call | solution.py:420
  2.1 4.2 %all-to-all-start = ((bf16[8,272,128]{2,1,0:T(8,128)(2,1)}), bf16[8,272,128]{2,1,0:T(8,128)(2,1)S(1)}, u32[]{:S(2)}, u32[]{:S(2)}) async-start(bf16[8,272,128]{2,1,0:T(8,128)(2,1)} %pack_kv.1), calls=%async_computation | async-start | bytes 1114112 | tf_op jit(solution)/shard_map/all_to_all | solution.py:416
  6.3 0.0 copy-done.3
  6.3 0.0 copy-done.2
  6.3 0.0 copy-done.1
  6.3 0.0 copy-done
  6.3 1.7 %pack_q.1 = (bf16[8,128,512]{2,1,0:T(8,128)(2,1)}, f32[3,16,128]{2,1,0:T(8,128)S(1)}, bf16[1024,128]{1,0:T(8,128)(2,1)S(1)}) custom-call(s32[1,16]{1,0:T(1,128)S(1)} %copy-done.3, s32[1,16]{1,0:T(1,128)S(1)} %copy-done.2, s32[1,16,64]{2,1,0:T(8,128)S(1)} %copy-done.1, bf16[1,1024,512]{2,1,0:T(8,128)(2,1)S(1)} %copy-done), custom_call_target="tpu_custom_call" | custom-call | bytes 2097152 | tf_op jit(solution)/shard_map/pack_q/pallas_call | solution.py:430
  8.1 6.0 %all-to-all-done.received = bf16[8,272,128]{2,1,0:T(8,128)(2,1)S(1)} async-done(((bf16[8,272,128]{2,1,0:T(8,128)(2,1)}), bf16[8,272,128]{2,1,0:T(8,128)(2,1)S(1)}, u32[]{:S(2)}, u32[]{:S(2)}) %all-to-all-start) | async-done | bytes 557088 | tf_op jit(solution)/shard_map/all_to_all | solution.py:416
  14.0 5.9 %all-to-all-start.1 = ((bf16[8,128,512]{2,1,0:T(8,128)(2,1)}), bf16[8,128,512]{2,1,0:T(8,128)(2,1)S(1)}, u32[]{:S(2)}, u32[]{:S(2)}) async-start(bf16[8,128,512]{2,1,0:T(8,128)(2,1)} %get-tuple-element.25), calls=%async_computation.1 | async-start | bytes 2097152 | tf_op jit(solution)/shard_map/all_to_all | solution.py:416
  19.9 0.7 %place_kv.1 = (bf16[1024,128]{1,0:T(8,128)(2,1)S(1)}, bf16[1024,128]{1,0:T(8,128)(2,1)S(1)}, s32[1,16]{1,0:T(1,128)S(1)}) custom-call(bf16[8,272,128]{2,1,0:T(8,128)(2,1)S(1)} %all-to-all-done.received), custom_call_target="tpu_custom_call" | custom-call | bytes 1048576 | tf_op jit(solution)/shard_map/place_kv/pallas_call | solution.py:446
  20.6 1.3 %collective-permute-start = (bf16[1024,128]{1,0:T(8,128)(2,1)S(1)}, bf16[1024,128]{1,0:T(8,128)(2,1)S(1)}, u32[]{:S(2)}, u32[]{:S(2)}) collective-permute-start(bf16[1024,128]{1,0:T(8,128)(2,1)S(1)} %get-tuple-element.26.early), channel_id=1, source_target_pairs={{0,1},{1,2},{2,3},{4,5},{5,6},{6,7},{8,9},{9,10},{10,11},{12,13},{... | collective-permute-start | bytes 786440 | tf_op jit(solution)/shard_map/ppermute | solution.py:29
  21.9 1.3 %collective-permute-start.2 = (bf16[1024,128]{1,0:T(8,128)(2,1)S(1)}, bf16[1024,128]{1,0:T(8,128)(2,1)S(1)}, u32[]{:S(2)}, u32[]{:S(2)}) collective-permute-start(bf16[1024,128]{1,0:T(8,128)(2,1)S(1)} %get-tuple-element.27.rest), channel_id=1, source_target_pairs={{0,1},{1,2},{2,3},{4,5},{5,6},{6,7},{8,9},{9,10},{10,11},{12,13},{... | collective-permute-start | bytes 786440 | tf_op jit(solution)/shard_map/ppermute | solution.py:29
  23.2 8.4 %collective-permute-done.early = bf16[1024,128]{1,0:T(8,128)(2,1)S(1)} collective-permute-done((bf16[1024,128]{1,0:T(8,128)(2,1)S(1)}, bf16[1024,128]{1,0:T(8,128)(2,1)S(1)}, u32[]{:S(2)}, u32[]{:S(2)}) %collective-permute-start) | collective-permute-done | bytes 262176 | tf_op jit(solution)/shard_map/ppermute | solution.py:29
  31.6 1.3 %collective-permute-start.1 = (bf16[1024,128]{1,0:T(8,128)(2,1)S(1)}, bf16[1024,128]{1,0:T(8,128)(2,1)S(1)}, u32[]{:S(2)}, u32[]{:S(2)}) collective-permute-start(bf16[1024,128]{1,0:T(8,128)(2,1)S(1)} %collective-permute-done.early), channel_id=1, source_target_pairs={{0,1},{1,2},{2,3},{4,5},{5,6},{6,7},{8,9},{9,10},{10,11},{12,13},{... | collective-permute-start | bytes 786440 | tf_op jit(solution)/shard_map/ppermute | solution.py:29
  32.9 0.1 all-to-all-done.1
  33.0 4.6 %attend_own.1 = (bf16[1,1024,512]{2,1,0:T(8,128)(2,1)}, f32[4096,256]{1,0:T(8,128)S(1)}, f32[4096,128]{1,0:T(8,128)S(1)}) custom-call(s32[1,16]{1,0:T(1,128)S(1)} %get-tuple-element.22.order, f32[3,16,128]{2,1,0:T(8,128)S(1)} %get-tuple-element.23.bias_in, bf16[1024,128]{1,0:T(8,128)(2,1)S(1)} %get-tuple-element.24.block_of, bf16[1024,512]{1,0:T(8,128)(2,1)S(1)} %bitcast.1, ...), custom_call_target="tpu_custom_call" | custom-call | flops 1073741824 | bytes 4194304 | tf_op jit(solution)/shard_map/attend_own/pallas_call | solution.py:482
  37.6 0.0 collective-permute-done.2.rest
  37.6 1.3 %collective-permute-start.3 = (bf16[1024,128]{1,0:T(8,128)(2,1)S(1)}, bf16[1024,128]{1,0:T(8,128)(2,1)S(1)}, u32[]{:S(2)}, u32[]{:S(2)}) collective-permute-start(bf16[1024,128]{1,0:T(8,128)(2,1)S(1)} %collective-permute-done.2.rest), channel_id=1, source_target_pairs={{0,1},{1,2},{2,3},{4,5},{5,6},{6,7},{8,9},{9,10},{10,11},{12,13},{... | collective-permute-start | bytes 786440 | tf_op jit(solution)/shard_map/ppermute | solution.py:29
  38.9 4.9 %attend_back_1.1 = (bf16[1,1024,512]{2,1,0:T(8,128)(2,1)}, f32[4096,128]{1,0:T(8,128)S(1)}, f32[4096,256]{1,0:T(8,128)S(1)}) custom-call(s32[1,16]{1,0:T(1,128)S(1)} %get-tuple-element.22.order, s32[1,16]{1,0:T(1,128)S(1)} %copy-done.2, f32[3,16,128]{2,1,0:T(8,128)S(1)} %get-tuple-element.23.bias_in, ...), custom_call_target="tpu_custom_call", output_to_operand_aliasing={{0}: (7, {}), {1}: (8, {})} | custom-call | flops 2147483648 | bytes 4194304 | tf_op jit(solution)/shard_map/attend_back_1/pallas_call | solution.py:468
  43.9 0.0 collective-permute-done.1.early
  43.9 3.8 %collective-permute-done.3.rest = bf16[1024,128]{1,0:T(8,128)(2,1)S(1)} collective-permute-done((bf16[1024,128]{1,0:T(8,128)(2,1)S(1)}, bf16[1024,128]{1,0:T(8,128)(2,1)S(1)}, u32[]{:S(2)}, u32[]{:S(2)}) %collective-permute-start.3) | collective-permute-done | bytes 262176 | tf_op jit(solution)/shard_map/ppermute | solution.py:29
  47.7 4.1 %attend_back_2.1 = (bf16[1,1024,512]{2,1,0:T(8,128)(2,1)}, f32[4096,128]{1,0:T(8,128)S(1)}) custom-call(s32[1,16]{1,0:T(1,128)S(1)} %get-tuple-element.22.order, s32[1,16]{1,0:T(1,128)S(1)} %copy-done.2, f32[3,16,128]{2,1,0:T(8,128)S(1)} %get-tuple-element.23.bias_in, ...), custom_call_target="tpu_custom_call", output_to_operand_aliasing={{0}: (7, {}), {1}: (8, {})} | custom-call | flops 2147483648 | bytes 4194304 | tf_op jit(solution)/shard_map/attend_back_2/pallas_call | solution.py:468
Async XLA Ops:
  0.0 6.3 %copy-start.3 = (s32[1,16]{1,0:T(1,128)S(1)}, s32[1,16]{1,0:T(1,128)}, u32[]{:S(2)}) copy-start(s32[1,16]{1,0:T(1,128)} %targets.3) | copy-start | bytes 196
  0.0 6.3 %copy-start.2 = (s32[1,16]{1,0:T(1,128)S(1)}, s32[1,16]{1,0:T(1,128)}, u32[]{:S(2)}) copy-start(s32[1,16]{1,0:T(1,128)} %lengths.5) | copy-start | bytes 196
  0.0 6.3 %copy-start.1 = (s32[1,16,64]{2,1,0:T(8,128)S(1)}, s32[1,16,64]{2,1,0:T(8,128)}, u32[]{:S(2)}) copy-start(s32[1,16,64]{2,1,0:T(8,128)} %tiles.1) | copy-start | bytes 12292
  0.0 6.3 %copy-start = (bf16[1,1024,512]{2,1,0:T(8,128)(2,1)S(1)}, bf16[1,1024,512]{2,1,0:T(8,128)(2,1)}, u32[]{:S(2)}) copy-start(bf16[1,1024,512]{2,1,0:T(8,128)(2,1)} %queries.1) | copy-start | bytes 3145732
  2.1 11.9 %all-to-all-start = ((bf16[8,272,128]{2,1,0:T(8,128)(2,1)}), bf16[8,272,128]{2,1,0:T(8,128)(2,1)S(1)}, u32[]{:S(2)}, u32[]{:S(2)}) async-start(bf16[8,272,128]{2,1,0:T(8,128)(2,1)} %pack_kv.1), calls=%async_computation | async-start | bytes 1114112 | tf_op jit(solution)/shard_map/all_to_all | solution.py:416
  14.0 18.9 %all-to-all-start.1 = ((bf16[8,128,512]{2,1,0:T(8,128)(2,1)}), bf16[8,128,512]{2,1,0:T(8,128)(2,1)S(1)}, u32[]{:S(2)}, u32[]{:S(2)}) async-start(bf16[8,128,512]{2,1,0:T(8,128)(2,1)} %get-tuple-element.25), calls=%async_computation.1 | async-start | bytes 2097152 | tf_op jit(solution)/shard_map/all_to_all | solution.py:416
  20.6 11.0 %collective-permute-start = (bf16[1024,128]{1,0:T(8,128)(2,1)S(1)}, bf16[1024,128]{1,0:T(8,128)(2,1)S(1)}, u32[]{:S(2)}, u32[]{:S(2)}) collective-permute-start(bf16[1024,128]{1,0:T(8,128)(2,1)S(1)} %get-tuple-element.26.early), channel_id=1, source_target_pairs={{0,1},{1,2},{2,3},{4,5},{5,6},{6,7},{8,9},{9,10},{10,11},{12,13},{... | collective-permute-start | bytes 786440 | tf_op jit(solution)/shard_map/ppermute | solution.py:29
  21.9 15.7 %collective-permute-start.2 = (bf16[1024,128]{1,0:T(8,128)(2,1)S(1)}, bf16[1024,128]{1,0:T(8,128)(2,1)S(1)}, u32[]{:S(2)}, u32[]{:S(2)}) collective-permute-start(bf16[1024,128]{1,0:T(8,128)(2,1)S(1)} %get-tuple-element.27.rest), channel_id=1, source_target_pairs={{0,1},{1,2},{2,3},{4,5},{5,6},{6,7},{8,9},{9,10},{10,11},{12,13},{... | collective-permute-start | bytes 786440 | tf_op jit(solution)/shard_map/ppermute | solution.py:29
  31.6 12.2 %collective-permute-start.1 = (bf16[1024,128]{1,0:T(8,128)(2,1)S(1)}, bf16[1024,128]{1,0:T(8,128)(2,1)S(1)}, u32[]{:S(2)}, u32[]{:S(2)}) collective-permute-start(bf16[1024,128]{1,0:T(8,128)(2,1)S(1)} %collective-permute-done.early), channel_id=1, source_target_pairs={{0,1},{1,2},{2,3},{4,5},{5,6},{6,7},{8,9},{9,10},{10,11},{12,13},{... | collective-permute-start | bytes 786440 | tf_op jit(solution)/shard_map/ppermute | solution.py:29
  37.6 10.1 %collective-permute-start.3 = (bf16[1024,128]{1,0:T(8,128)(2,1)S(1)}, bf16[1024,128]{1,0:T(8,128)(2,1)S(1)}, u32[]{:S(2)}, u32[]{:S(2)}) collective-permute-start(bf16[1024,128]{1,0:T(8,128)(2,1)S(1)} %collective-permute-done.2.rest), channel_id=1, source_target_pairs={{0,1},{1,2},{2,3},{4,5},{5,6},{6,7},{8,9},{9,10},{10,11},{12,13},{... | collective-permute-start | bytes 786440 | tf_op jit(solution)/shard_map/ppermute | solution.py:29
where the time goes:
time: 52.3 us; the launch traced here: 52 us
  waiting for transfers between devices  18.3 us (35%)
  Pallas kernels  18.2 us (35%)
  starting transfers between devices  15.2 us (29%)
    ppermute x4, waiting for transfers between devices, shifted(): lax.ppermute(value, axis, [(source, source + 1) for source in range(count...  12.3 us
    all_to_all x2, starting transfers between devices, route(): return lax.all_to_all(sent, 'dp', split_axis=0, concat_axis=0, tiled=True)  10.1 us
    pallas_call x2, Pallas kernels, attend_back(): pl.pallas_call(functools.partial(hop_kernel, offset), out_shape=(out_shap...  9.04 us
    all_to_all x2, waiting for transfers between devices, route(): return lax.all_to_all(sent, 'dp', split_axis=0, concat_axis=0, tiled=True)  6.05 us
    ppermute x4, starting transfers between devices, shifted(): lax.ppermute(value, axis, [(source, source + 1) for source in range(count...  5.16 us
    pallas_call x1, Pallas kernels, per_device(): pl.pallas_call(own_kernel, out_shape=(out_shape, sums_shape, level_shape)...  4.63 us
    pallas_call x1, Pallas kernels, per_device(): pl.pallas_call(functools.partial(pack_kv_kernel, cap), out_shape=jax.Shap...  2.09 us
    pallas_call x1, Pallas kernels, per_device(): pl.pallas_call(functools.partial(pack_q_kernel, cap), out_shape=(jax.Shap...  1.72 us
  transfers between devices with their start and end apart: 6, of which 4 were waited for; matrix products, arithmetic and copies ran while one was open for 0% of the time, Pallas kernels for 23%

commit v1 on v0

--- a/solution.py
+++ b/solution.py
@@ -15,7 +15,7 @@
 CHUNK = 256
 SLOT_ROWS = 16
 REACH = 2
-PIECE = 4
+PIECE = 3
 VMEM_LIMIT = 32 * 1024 * 1024
 VMEM_SMALL = 8 * 1024 * 1024
 

time: 52.3 us -> 58 us (1.11)
  the two profiles are of different devices: /device:TPU:30 before, /device:TPU:19 now
where the time goes in v1:
time: 58 us; the launch traced here: 57.3 us
  waiting for transfers between devices  21 us (36%)
  starting transfers between devices  19.8 us (34%)
  Pallas kernels  16.2 us (28%)
    all_to_all x2, waiting for transfers between devices, route(): return lax.all_to_all(sent, 'dp', split_axis=0, concat_axis=0, tiled=True)  14.8 us
    ppermute x4, starting transfers between devices, shifted(): lax.ppermute(value, axis, [(source, source + 1) for source in range(count...  10.2 us
    all_to_all x2, starting transfers between devices, route(): return lax.all_to_all(sent, 'dp', split_axis=0, concat_axis=0, tiled=True)  9.58 us
    pallas_call x2, Pallas kernels, attend_back(): pl.pallas_call(functools.partial(hop_kernel, offset), out_shape=(out_shap...  7.11 us
    ppermute x4, waiting for transfers between devices, shifted(): lax.ppermute(value, axis, [(source, source + 1) for source in range(count...  6.17 us
    pallas_call x1, Pallas kernels, per_device(): pl.pallas_call(own_kernel, out_shape=(out_shape, sums_shape, level_shape)...  4.63 us
    pallas_call x1, Pallas kernels, per_device(): pl.pallas_call(functools.partial(pack_kv_kernel, cap), out_shape=jax.Shap...  2.09 us
    pallas_call x1, Pallas kernels, per_device(): pl.pallas_call(functools.partial(pack_q_kernel, cap), out_shape=(jax.Shap...  1.72 us
  transfers between devices with their start and end apart: 6, of which 3 were waited for; matrix products, arithmetic and copies ran while one was open for 0% of the time, Pallas kernels for 19%

profile of v1, /device:TPU:19, one launch (start us, length us, event | category | flops | bytes accessed | tf_op | source)
XLA Modules:
  0.0 57.3 jit_solution(3480132933607809810)
XLA Ops:
  0.0 0.0 copy-start.3
  0.0 0.0 copy-start.2
  0.0 0.0 copy-start.1
  0.0 0.0 copy-start
  0.0 2.1 %pack_kv.1 = bf16[8,272,128]{2,1,0:T(8,128)(2,1)} custom-call(s32[1,16]{1,0:T(1,128)} %targets.3, s32[1,16]{1,0:T(1,128)} %slots.1, bf16[1,1024,128]{2,1,0:T(8,128)(2,1)} %keys.1, bf16[1,1024,128]{2,1,0:T(8,128)(2,1)} %values.1), custom_call_target="tpu_custom_call" | custom-call | bytes 1048576 | tf_op jit(solution)/shard_map/pack_kv/pallas_call | solution.py:420
  2.1 4.6 %all-to-all-start = ((bf16[8,272,128]{2,1,0:T(8,128)(2,1)}), bf16[8,272,128]{2,1,0:T(8,128)(2,1)S(1)}, u32[]{:S(2)}, u32[]{:S(2)}) async-start(bf16[8,272,128]{2,1,0:T(8,128)(2,1)} %pack_kv.1), calls=%async_computation | async-start | bytes 1114112 | tf_op jit(solution)/shard_map/all_to_all | solution.py:416
  6.7 0.0 copy-done.3
  6.7 0.0 copy-done.2
  6.7 0.0 copy-done.1
  6.7 0.0 copy-done
  6.7 1.7 %pack_q.1 = (bf16[8,128,512]{2,1,0:T(8,128)(2,1)}, f32[3,16,128]{2,1,0:T(8,128)S(1)}, bf16[1024,128]{1,0:T(8,128)(2,1)S(1)}) custom-call(s32[1,16]{1,0:T(1,128)S(1)} %copy-done.3, s32[1,16]{1,0:T(1,128)S(1)} %copy-done.2, s32[1,16,64]{2,1,0:T(8,128)S(1)} %copy-done.1, bf16[1,1024,512]{2,1,0:T(8,128)(2,1)S(1)} %copy-done), custom_call_target="tpu_custom_call" | custom-call | bytes 2097152 | tf_op jit(solution)/shard_map/pack_q/pallas_call | solution.py:430
  8.4 6.8 %all-to-all-done.received = bf16[8,272,128]{2,1,0:T(8,128)(2,1)S(1)} async-done(((bf16[8,272,128]{2,1,0:T(8,128)(2,1)}), bf16[8,272,128]{2,1,0:T(8,128)(2,1)S(1)}, u32[]{:S(2)}, u32[]{:S(2)}) %all-to-all-start) | async-done | bytes 557088 | tf_op jit(solution)/shard_map/all_to_all | solution.py:416
  15.2 5.0 %all-to-all-start.1 = ((bf16[8,128,512]{2,1,0:T(8,128)(2,1)}), bf16[8,128,512]{2,1,0:T(8,128)(2,1)S(1)}, u32[]{:S(2)}, u32[]{:S(2)}) async-start(bf16[8,128,512]{2,1,0:T(8,128)(2,1)} %get-tuple-element.25), calls=%async_computation.1 | async-start | bytes 2097152 | tf_op jit(solution)/shard_map/all_to_all | solution.py:416
  20.3 0.7 %place_kv.1 = (bf16[768,128]{1,0:T(8,128)(2,1)S(1)}, bf16[1280,128]{1,0:T(8,128)(2,1)S(1)}, s32[1,16]{1,0:T(1,128)S(1)}) custom-call(bf16[8,272,128]{2,1,0:T(8,128)(2,1)S(1)} %all-to-all-done.received), custom_call_target="tpu_custom_call" | custom-call | bytes 1048576 | tf_op jit(solution)/shard_map/place_kv/pallas_call | solution.py:446
  20.9 3.2 %collective-permute-start.2 = (bf16[1280,128]{1,0:T(8,128)(2,1)S(1)}, bf16[1280,128]{1,0:T(8,128)(2,1)S(1)}, u32[]{:S(2)}, u32[]{:S(2)}) collective-permute-start(bf16[1280,128]{1,0:T(8,128)(2,1)S(1)} %get-tuple-element.27.rest), channel_id=1, source_target_pairs={{0,1},{1,2},{2,3},{4,5},{5,6},{6,7},{8,9},{9,10},{10,11},{12,13},{... | collective-permute-start | bytes 983048 | tf_op jit(solution)/shard_map/ppermute | solution.py:29
  24.1 1.9 %collective-permute-start = (bf16[768,128]{1,0:T(8,128)(2,1)S(1)}, bf16[768,128]{1,0:T(8,128)(2,1)S(1)}, u32[]{:S(2)}, u32[]{:S(2)}) collective-permute-start(bf16[768,128]{1,0:T(8,128)(2,1)S(1)} %get-tuple-element.26.early), channel_id=1, source_target_pairs={{0,1},{1,2},{2,3},{4,5},{5,6},{6,7},{8,9},{9,10},{10,11},{12,13},{... | collective-permute-start | bytes 589832 | tf_op jit(solution)/shard_map/ppermute | solution.py:29
  26.1 8.0 %all-to-all-done.1 = bf16[8,128,512]{2,1,0:T(8,128)(2,1)S(1)} async-done(((bf16[8,128,512]{2,1,0:T(8,128)(2,1)}), bf16[8,128,512]{2,1,0:T(8,128)(2,1)S(1)}, u32[]{:S(2)}, u32[]{:S(2)}) %all-to-all-start.1) | async-done | bytes 1048608 | tf_op jit(solution)/shard_map/all_to_all | solution.py:416
  34.1 4.6 %attend_own.1 = (bf16[1,1024,512]{2,1,0:T(8,128)(2,1)}, f32[4096,256]{1,0:T(8,128)S(1)}, f32[4096,128]{1,0:T(8,128)S(1)}) custom-call(s32[1,16]{1,0:T(1,128)S(1)} %get-tuple-element.22.order, f32[3,16,128]{2,1,0:T(8,128)S(1)} %get-tuple-element.23.bias_in, bf16[1024,128]{1,0:T(8,128)(2,1)S(1)} %get-tuple-element.24.block_of, bf16[1024,512]{1,0:T(8,128)(2,1)S(1)} %bitcast.1, ...), custom_call_target="tpu_custom_call" | custom-call | flops 1073741824 | bytes 4194304 | tf_op jit(solution)/shard_map/attend_own/pallas_call | solution.py:482
  38.7 0.0 collective-permute-done.2.rest
  38.7 3.2 %collective-permute-start.3 = (bf16[1280,128]{1,0:T(8,128)(2,1)S(1)}, bf16[1280,128]{1,0:T(8,128)(2,1)S(1)}, u32[]{:S(2)}, u32[]{:S(2)}) collective-permute-start(bf16[1280,128]{1,0:T(8,128)(2,1)S(1)} %collective-permute-done.2.rest), channel_id=1, source_target_pairs={{0,1},{1,2},{2,3},{4,5},{5,6},{6,7},{8,9},{9,10},{10,11},{12,13},{... | collective-permute-start | bytes 983048 | tf_op jit(solution)/shard_map/ppermute | solution.py:29
  41.9 0.0 collective-permute-done.early
  42.0 1.9 %collective-permute-start.1 = (bf16[768,128]{1,0:T(8,128)(2,1)S(1)}, bf16[768,128]{1,0:T(8,128)(2,1)S(1)}, u32[]{:S(2)}, u32[]{:S(2)}) collective-permute-start(bf16[768,128]{1,0:T(8,128)(2,1)S(1)} %collective-permute-done.early), channel_id=1, source_target_pairs={{0,1},{1,2},{2,3},{4,5},{5,6},{6,7},{8,9},{9,10},{10,11},{12,13},{... | collective-permute-start | bytes 589832 | tf_op jit(solution)/shard_map/ppermute | solution.py:29
  43.9 3.6 %attend_back_1.1 = (bf16[1,1024,512]{2,1,0:T(8,128)(2,1)}, f32[4096,128]{1,0:T(8,128)S(1)}, f32[4096,256]{1,0:T(8,128)S(1)}) custom-call(s32[1,16]{1,0:T(1,128)S(1)} %get-tuple-element.22.order, s32[1,16]{1,0:T(1,128)S(1)} %copy-done.2, f32[3,16,128]{2,1,0:T(8,128)S(1)} %get-tuple-element.23.bias_in, ...), custom_call_target="tpu_custom_call", output_to_operand_aliasing={{0}: (7, {}), {1}: (8, {})} | custom-call | flops 2147483648 | bytes 4194304 | tf_op jit(solution)/shard_map/attend_back_1/pallas_call | solution.py:468
  47.5 6.2 %collective-permute-done.1.early = bf16[768,128]{1,0:T(8,128)(2,1)S(1)} collective-permute-done((bf16[768,128]{1,0:T(8,128)(2,1)S(1)}, bf16[768,128]{1,0:T(8,128)(2,1)S(1)}, u32[]{:S(2)}, u32[]{:S(2)}) %collective-permute-start.1) | collective-permute-done | bytes 196640 | tf_op jit(solution)/shard_map/ppermute | solution.py:29
  53.7 0.0 collective-permute-done.3.rest
  53.7 3.5 %attend_back_2.1 = (bf16[1,1024,512]{2,1,0:T(8,128)(2,1)}, f32[4096,128]{1,0:T(8,128)S(1)}) custom-call(s32[1,16]{1,0:T(1,128)S(1)} %get-tuple-element.22.order, s32[1,16]{1,0:T(1,128)S(1)} %copy-done.2, f32[3,16,128]{2,1,0:T(8,128)S(1)} %get-tuple-element.23.bias_in, ...), custom_call_target="tpu_custom_call", output_to_operand_aliasing={{0}: (7, {}), {1}: (8, {})} | custom-call | flops 2147483648 | bytes 4194304 | tf_op jit(solution)/shard_map/attend_back_2/pallas_call | solution.py:468
Async XLA Ops:
  0.0 6.7 %copy-start.3 = (s32[1,16]{1,0:T(1,128)S(1)}, s32[1,16]{1,0:T(1,128)}, u32[]{:S(2)}) copy-start(s32[1,16]{1,0:T(1,128)} %targets.3) | copy-start | bytes 196
  0.0 6.7 %copy-start.2 = (s32[1,16]{1,0:T(1,128)S(1)}, s32[1,16]{1,0:T(1,128)}, u32[]{:S(2)}) copy-start(s32[1,16]{1,0:T(1,128)} %lengths.5) | copy-start | bytes 196
  0.0 6.7 %copy-start.1 = (s32[1,16,64]{2,1,0:T(8,128)S(1)}, s32[1,16,64]{2,1,0:T(8,128)}, u32[]{:S(2)}) copy-start(s32[1,16,64]{2,1,0:T(8,128)} %tiles.1) | copy-start | bytes 12292
  0.0 6.7 %copy-start = (bf16[1,1024,512]{2,1,0:T(8,128)(2,1)S(1)}, bf16[1,1024,512]{2,1,0:T(8,128)(2,1)}, u32[]{:S(2)}) copy-start(bf16[1,1024,512]{2,1,0:T(8,128)(2,1)} %queries.1) | copy-start | bytes 3145732
  2.1 13.1 %all-to-all-start = ((bf16[8,272,128]{2,1,0:T(8,128)(2,1)}), bf16[8,272,128]{2,1,0:T(8,128)(2,1)S(1)}, u32[]{:S(2)}, u32[]{:S(2)}) async-start(bf16[8,272,128]{2,1,0:T(8,128)(2,1)} %pack_kv.1), calls=%async_computation | async-start | bytes 1114112 | tf_op jit(solution)/shard_map/all_to_all | solution.py:416
  15.2 18.8 %all-to-all-start.1 = ((bf16[8,128,512]{2,1,0:T(8,128)(2,1)}), bf16[8,128,512]{2,1,0:T(8,128)(2,1)S(1)}, u32[]{:S(2)}, u32[]{:S(2)}) async-start(bf16[8,128,512]{2,1,0:T(8,128)(2,1)} %get-tuple-element.25), calls=%async_computation.1 | async-start | bytes 2097152 | tf_op jit(solution)/shard_map/all_to_all | solution.py:416
  20.9 17.8 %collective-permute-start.2 = (bf16[1280,128]{1,0:T(8,128)(2,1)S(1)}, bf16[1280,128]{1,0:T(8,128)(2,1)S(1)}, u32[]{:S(2)}, u32[]{:S(2)}) collective-permute-start(bf16[1280,128]{1,0:T(8,128)(2,1)S(1)} %get-tuple-element.27.rest), channel_id=1, source_target_pairs={{0,1},{1,2},{2,3},{4,5},{5,6},{6,7},{8,9},{9,10},{10,11},{12,13},{... | collective-permute-start | bytes 983048 | tf_op jit(solution)/shard_map/ppermute | solution.py:29
  24.1 17.8 %collective-permute-start = (bf16[768,128]{1,0:T(8,128)(2,1)S(1)}, bf16[768,128]{1,0:T(8,128)(2,1)S(1)}, u32[]{:S(2)}, u32[]{:S(2)}) collective-permute-start(bf16[768,128]{1,0:T(8,128)(2,1)S(1)} %get-tuple-element.26.early), channel_id=1, source_target_pairs={{0,1},{1,2},{2,3},{4,5},{5,6},{6,7},{8,9},{9,10},{10,11},{12,13},{... | collective-permute-start | bytes 589832 | tf_op jit(solution)/shard_map/ppermute | solution.py:29
  38.7 15.0 %collective-permute-start.3 = (bf16[1280,128]{1,0:T(8,128)(2,1)S(1)}, bf16[1280,128]{1,0:T(8,128)(2,1)S(1)}, u32[]{:S(2)}, u32[]{:S(2)}) collective-permute-start(bf16[1280,128]{1,0:T(8,128)(2,1)S(1)} %collective-permute-done.2.rest), channel_id=1, source_target_pairs={{0,1},{1,2},{2,3},{4,5},{5,6},{6,7},{8,9},{9,10},{10,11},{12,13},{... | collective-permute-start | bytes 983048 | tf_op jit(solution)/shard_map/ppermute | solution.py:29
  42.0 11.7 %collective-permute-start.1 = (bf16[768,128]{1,0:T(8,128)(2,1)S(1)}, bf16[768,128]{1,0:T(8,128)(2,1)S(1)}, u32[]{:S(2)}, u32[]{:S(2)}) collective-permute-start(bf16[768,128]{1,0:T(8,128)(2,1)S(1)} %collective-permute-done.early), channel_id=1, source_target_pairs={{0,1},{1,2},{2,3},{4,5},{5,6},{6,7},{8,9},{9,10},{10,11},{12,13},{... | collective-permute-start | bytes 589832 | tf_op jit(solution)/shard_map/ppermute | solution.py:29

commit v2 on v0

--- a/solution.py
+++ b/solution.py
@@ -391,7 +391,7 @@
     if offset < REACH:
         more, _ = reach_of(lengths, place, offset + 1, blocks)
         pl.when((reads > 0) & (more > 0))(functools.partial(over, 0, 4, False))
-    for n, together in enumerate((4, 4, 8, 8)):
+    for n, together in enumerate((8 if offset < REACH else 4, 4, 8, 8)):
         pl.when((reads > 0) & (more == 0) & (part == n))(
             functools.partial(over, n * (tokens // 4), together, True)
         )

time: 52.3 us -> 51.7 us (0.989)
  the two profiles are of different devices: /device:TPU:30 before, /device:TPU:24 now
where the time goes in v2:
time: 51.7 us; the launch traced here: 51 us
  waiting for transfers between devices  19.8 us (38%)
  Pallas kernels  18.5 us (36%)
  starting transfers between devices  12.4 us (24%)
    all_to_all x2, waiting for transfers between devices, route(): return lax.all_to_all(sent, 'dp', split_axis=0, concat_axis=0, tiled=True)  10.7 us
    pallas_call x2, Pallas kernels, attend_back(): pl.pallas_call(functools.partial(hop_kernel, offset), out_shape=(out_shap...  9.34 us
    ppermute x4, waiting for transfers between devices, shifted(): lax.ppermute(value, axis, [(source, source + 1) for source in range(count...  9.06 us
    all_to_all x2, starting transfers between devices, route(): return lax.all_to_all(sent, 'dp', split_axis=0, concat_axis=0, tiled=True)  7.28 us
    ppermute x4, starting transfers between devices, shifted(): lax.ppermute(value, axis, [(source, source + 1) for source in range(count...  5.16 us
    pallas_call x1, Pallas kernels, per_device(): pl.pallas_call(own_kernel, out_shape=(out_shape, sums_shape, level_shape)...  4.63 us
    pallas_call x1, Pallas kernels, per_device(): pl.pallas_call(functools.partial(pack_kv_kernel, cap), out_shape=jax.Shap...  2.09 us
    pallas_call x1, Pallas kernels, per_device(): pl.pallas_call(functools.partial(pack_q_kernel, cap), out_shape=(jax.Shap...  1.72 us
  transfers between devices with their start and end apart: 6, of which 4 were waited for; matrix products, arithmetic and copies ran while one was open for 0% of the time, Pallas kernels for 26%

profile of v2, /device:TPU:24, one launch (start us, length us, event | category | flops | bytes accessed | tf_op | source)
XLA Modules:
  0.0 51.0 jit_solution(16286883214993256870)
XLA Ops:
  0.0 0.0 copy-start.3
  0.0 0.0 copy-start.2
  0.0 0.0 copy-start.1
  0.0 0.0 copy-start
  0.0 2.1 %pack_kv.1 = bf16[8,272,128]{2,1,0:T(8,128)(2,1)} custom-call(s32[1,16]{1,0:T(1,128)} %targets.3, s32[1,16]{1,0:T(1,128)} %slots.1, bf16[1,1024,128]{2,1,0:T(8,128)(2,1)} %keys.1, bf16[1,1024,128]{2,1,0:T(8,128)(2,1)} %values.1), custom_call_target="tpu_custom_call" | custom-call | bytes 1048576 | tf_op jit(solution)/shard_map/pack_kv/pallas_call | solution.py:420
  2.1 3.7 %all-to-all-start = ((bf16[8,272,128]{2,1,0:T(8,128)(2,1)}), bf16[8,272,128]{2,1,0:T(8,128)(2,1)S(1)}, u32[]{:S(2)}, u32[]{:S(2)}) async-start(bf16[8,272,128]{2,1,0:T(8,128)(2,1)} %pack_kv.1), calls=%async_computation | async-start | bytes 1114112 | tf_op jit(solution)/shard_map/all_to_all | solution.py:416
  5.8 0.0 copy-done.3
  5.8 0.0 copy-done.2
  5.9 0.0 copy-done.1
  5.9 0.0 copy-done
  5.9 1.7 %pack_q.1 = (bf16[8,128,512]{2,1,0:T(8,128)(2,1)}, f32[3,16,128]{2,1,0:T(8,128)S(1)}, bf16[1024,128]{1,0:T(8,128)(2,1)S(1)}) custom-call(s32[1,16]{1,0:T(1,128)S(1)} %copy-done.3, s32[1,16]{1,0:T(1,128)S(1)} %copy-done.2, s32[1,16,64]{2,1,0:T(8,128)S(1)} %copy-done.1, bf16[1,1024,512]{2,1,0:T(8,128)(2,1)S(1)} %copy-done), custom_call_target="tpu_custom_call" | custom-call | bytes 2097152 | tf_op jit(solution)/shard_map/pack_q/pallas_call | solution.py:430
  7.6 8.3 %all-to-all-done.received = bf16[8,272,128]{2,1,0:T(8,128)(2,1)S(1)} async-done(((bf16[8,272,128]{2,1,0:T(8,128)(2,1)}), bf16[8,272,128]{2,1,0:T(8,128)(2,1)S(1)}, u32[]{:S(2)}, u32[]{:S(2)}) %all-to-all-start) | async-done | bytes 557088 | tf_op jit(solution)/shard_map/all_to_all | solution.py:416
  15.9 3.6 %all-to-all-start.1 = ((bf16[8,128,512]{2,1,0:T(8,128)(2,1)}), bf16[8,128,512]{2,1,0:T(8,128)(2,1)S(1)}, u32[]{:S(2)}, u32[]{:S(2)}) async-start(bf16[8,128,512]{2,1,0:T(8,128)(2,1)} %get-tuple-element.25), calls=%async_computation.1 | async-start | bytes 2097152 | tf_op jit(solution)/shard_map/all_to_all | solution.py:416
  19.5 0.7 %place_kv.1 = (bf16[1024,128]{1,0:T(8,128)(2,1)S(1)}, bf16[1024,128]{1,0:T(8,128)(2,1)S(1)}, s32[1,16]{1,0:T(1,128)S(1)}) custom-call(bf16[8,272,128]{2,1,0:T(8,128)(2,1)S(1)} %all-to-all-done.received), custom_call_target="tpu_custom_call" | custom-call | bytes 1048576 | tf_op jit(solution)/shard_map/place_kv/pallas_call | solution.py:446
  20.2 1.3 %collective-permute-start = (bf16[1024,128]{1,0:T(8,128)(2,1)S(1)}, bf16[1024,128]{1,0:T(8,128)(2,1)S(1)}, u32[]{:S(2)}, u32[]{:S(2)}) collective-permute-start(bf16[1024,128]{1,0:T(8,128)(2,1)S(1)} %get-tuple-element.26.early), channel_id=1, source_target_pairs={{0,1},{1,2},{2,3},{4,5},{5,6},{6,7},{8,9},{9,10},{10,11},{12,13},{... | collective-permute-start | bytes 786440 | tf_op jit(solution)/shard_map/ppermute | solution.py:29
  21.5 1.3 %collective-permute-start.2 = (bf16[1024,128]{1,0:T(8,128)(2,1)S(1)}, bf16[1024,128]{1,0:T(8,128)(2,1)S(1)}, u32[]{:S(2)}, u32[]{:S(2)}) collective-permute-start(bf16[1024,128]{1,0:T(8,128)(2,1)S(1)} %get-tuple-element.27.rest), channel_id=1, source_target_pairs={{0,1},{1,2},{2,3},{4,5},{5,6},{6,7},{8,9},{9,10},{10,11},{12,13},{... | collective-permute-start | bytes 786440 | tf_op jit(solution)/shard_map/ppermute | solution.py:29
  22.8 8.4 %collective-permute-done.early = bf16[1024,128]{1,0:T(8,128)(2,1)S(1)} collective-permute-done((bf16[1024,128]{1,0:T(8,128)(2,1)S(1)}, bf16[1024,128]{1,0:T(8,128)(2,1)S(1)}, u32[]{:S(2)}, u32[]{:S(2)}) %collective-permute-start) | collective-permute-done | bytes 262176 | tf_op jit(solution)/shard_map/ppermute | solution.py:29
  31.2 1.3 %collective-permute-start.1 = (bf16[1024,128]{1,0:T(8,128)(2,1)S(1)}, bf16[1024,128]{1,0:T(8,128)(2,1)S(1)}, u32[]{:S(2)}, u32[]{:S(2)}) collective-permute-start(bf16[1024,128]{1,0:T(8,128)(2,1)S(1)} %collective-permute-done.early), channel_id=1, source_target_pairs={{0,1},{1,2},{2,3},{4,5},{5,6},{6,7},{8,9},{9,10},{10,11},{12,13},{... | collective-permute-start | bytes 786440 | tf_op jit(solution)/shard_map/ppermute | solution.py:29
  32.5 2.4 %all-to-all-done.1 = bf16[8,128,512]{2,1,0:T(8,128)(2,1)S(1)} async-done(((bf16[8,128,512]{2,1,0:T(8,128)(2,1)}), bf16[8,128,512]{2,1,0:T(8,128)(2,1)S(1)}, u32[]{:S(2)}, u32[]{:S(2)}) %all-to-all-start.1) | async-done | bytes 1048608 | tf_op jit(solution)/shard_map/all_to_all | solution.py:416
  34.8 4.6 %attend_own.1 = (bf16[1,1024,512]{2,1,0:T(8,128)(2,1)}, f32[4096,256]{1,0:T(8,128)S(1)}, f32[4096,128]{1,0:T(8,128)S(1)}) custom-call(s32[1,16]{1,0:T(1,128)S(1)} %get-tuple-element.22.order, f32[3,16,128]{2,1,0:T(8,128)S(1)} %get-tuple-element.23.bias_in, bf16[1024,128]{1,0:T(8,128)(2,1)S(1)} %get-tuple-element.24.block_of, bf16[1024,512]{1,0:T(8,128)(2,1)S(1)} %bitcast.1, ...), custom_call_target="tpu_custom_call" | custom-call | flops 1073741824 | bytes 4194304 | tf_op jit(solution)/shard_map/attend_own/pallas_call | solution.py:482
  39.5 0.0 collective-permute-done.2.rest
  39.5 1.3 %collective-permute-start.3 = (bf16[1024,128]{1,0:T(8,128)(2,1)S(1)}, bf16[1024,128]{1,0:T(8,128)(2,1)S(1)}, u32[]{:S(2)}, u32[]{:S(2)}) collective-permute-start(bf16[1024,128]{1,0:T(8,128)(2,1)S(1)} %collective-permute-done.2.rest), channel_id=1, source_target_pairs={{0,1},{1,2},{2,3},{4,5},{5,6},{6,7},{8,9},{9,10},{10,11},{12,13},{... | collective-permute-start | bytes 786440 | tf_op jit(solution)/shard_map/ppermute | solution.py:29
  40.8 6.3 %attend_back_1.1 = (bf16[1,1024,512]{2,1,0:T(8,128)(2,1)}, f32[4096,128]{1,0:T(8,128)S(1)}, f32[4096,256]{1,0:T(8,128)S(1)}) custom-call(s32[1,16]{1,0:T(1,128)S(1)} %get-tuple-element.22.order, s32[1,16]{1,0:T(1,128)S(1)} %copy-done.2, f32[3,16,128]{2,1,0:T(8,128)S(1)} %get-tuple-element.23.bias_in, ...), custom_call_target="tpu_custom_call", output_to_operand_aliasing={{0}: (7, {}), {1}: (8, {})} | custom-call | flops 2147483648 | bytes 4194304 | tf_op jit(solution)/shard_map/attend_back_1/pallas_call | solution.py:468
  47.1 0.0 collective-permute-done.1.early
  47.1 0.7 %collective-permute-done.3.rest = bf16[1024,128]{1,0:T(8,128)(2,1)S(1)} collective-permute-done((bf16[1024,128]{1,0:T(8,128)(2,1)S(1)}, bf16[1024,128]{1,0:T(8,128)(2,1)S(1)}, u32[]{:S(2)}, u32[]{:S(2)}) %collective-permute-start.3) | collective-permute-done | bytes 262176 | tf_op jit(solution)/shard_map/ppermute | solution.py:29
  47.8 3.0 %attend_back_2.1 = (bf16[1,1024,512]{2,1,0:T(8,128)(2,1)}, f32[4096,128]{1,0:T(8,128)S(1)}) custom-call(s32[1,16]{1,0:T(1,128)S(1)} %get-tuple-element.22.order, s32[1,16]{1,0:T(1,128)S(1)} %copy-done.2, f32[3,16,128]{2,1,0:T(8,128)S(1)} %get-tuple-element.23.bias_in, ...), custom_call_target="tpu_custom_call", output_to_operand_aliasing={{0}: (7, {}), {1}: (8, {})} | custom-call | flops 2147483648 | bytes 4194304 | tf_op jit(solution)/shard_map/attend_back_2/pallas_call | solution.py:468
Async XLA Ops:
  0.0 5.8 %copy-start.3 = (s32[1,16]{1,0:T(1,128)S(1)}, s32[1,16]{1,0:T(1,128)}, u32[]{:S(2)}) copy-start(s32[1,16]{1,0:T(1,128)} %targets.3) | copy-start | bytes 196
  0.0 5.8 %copy-start.2 = (s32[1,16]{1,0:T(1,128)S(1)}, s32[1,16]{1,0:T(1,128)}, u32[]{:S(2)}) copy-start(s32[1,16]{1,0:T(1,128)} %lengths.5) | copy-start | bytes 196
  0.0 5.8 %copy-start.1 = (s32[1,16,64]{2,1,0:T(8,128)S(1)}, s32[1,16,64]{2,1,0:T(8,128)}, u32[]{:S(2)}) copy-start(s32[1,16,64]{2,1,0:T(8,128)} %tiles.1) | copy-start | bytes 12292
  0.0 5.9 %copy-start = (bf16[1,1024,512]{2,1,0:T(8,128)(2,1)S(1)}, bf16[1,1024,512]{2,1,0:T(8,128)(2,1)}, u32[]{:S(2)}) copy-start(bf16[1,1024,512]{2,1,0:T(8,128)(2,1)} %queries.1) | copy-start | bytes 3145732
  2.1 13.8 %all-to-all-start = ((bf16[8,272,128]{2,1,0:T(8,128)(2,1)}), bf16[8,272,128]{2,1,0:T(8,128)(2,1)S(1)}, u32[]{:S(2)}, u32[]{:S(2)}) async-start(bf16[8,272,128]{2,1,0:T(8,128)(2,1)} %pack_kv.1), calls=%async_computation | async-start | bytes 1114112 | tf_op jit(solution)/shard_map/all_to_all | solution.py:416
  15.9 18.9 %all-to-all-start.1 = ((bf16[8,128,512]{2,1,0:T(8,128)(2,1)}), bf16[8,128,512]{2,1,0:T(8,128)(2,1)S(1)}, u32[]{:S(2)}, u32[]{:S(2)}) async-start(bf16[8,128,512]{2,1,0:T(8,128)(2,1)} %get-tuple-element.25), calls=%async_computation.1 | async-start | bytes 2097152 | tf_op jit(solution)/shard_map/all_to_all | solution.py:416
  20.2 11.0 %collective-permute-start = (bf16[1024,128]{1,0:T(8,128)(2,1)S(1)}, bf16[1024,128]{1,0:T(8,128)(2,1)S(1)}, u32[]{:S(2)}, u32[]{:S(2)}) collective-permute-start(bf16[1024,128]{1,0:T(8,128)(2,1)S(1)} %get-tuple-element.26.early), channel_id=1, source_target_pairs={{0,1},{1,2},{2,3},{4,5},{5,6},{6,7},{8,9},{9,10},{10,11},{12,13},{... | collective-permute-start | bytes 786440 | tf_op jit(solution)/shard_map/ppermute | solution.py:29
  21.5 18.0 %collective-permute-start.2 = (bf16[1024,128]{1,0:T(8,128)(2,1)S(1)}, bf16[1024,128]{1,0:T(8,128)(2,1)S(1)}, u32[]{:S(2)}, u32[]{:S(2)}) collective-permute-start(bf16[1024,128]{1,0:T(8,128)(2,1)S(1)} %get-tuple-element.27.rest), channel_id=1, source_target_pairs={{0,1},{1,2},{2,3},{4,5},{5,6},{6,7},{8,9},{9,10},{10,11},{12,13},{... | collective-permute-start | bytes 786440 | tf_op jit(solution)/shard_map/ppermute | solution.py:29
  31.2 15.9 %collective-permute-start.1 = (bf16[1024,128]{1,0:T(8,128)(2,1)S(1)}, bf16[1024,128]{1,0:T(8,128)(2,1)S(1)}, u32[]{:S(2)}, u32[]{:S(2)}) collective-permute-start(bf16[1024,128]{1,0:T(8,128)(2,1)S(1)} %collective-permute-done.early), channel_id=1, source_target_pairs={{0,1},{1,2},{2,3},{4,5},{5,6},{6,7},{8,9},{9,10},{10,11},{12,13},{... | collective-permute-start | bytes 786440 | tf_op jit(solution)/shard_map/ppermute | solution.py:29
  39.5 8.3 %collective-permute-start.3 = (bf16[1024,128]{1,0:T(8,128)(2,1)S(1)}, bf16[1024,128]{1,0:T(8,128)(2,1)S(1)}, u32[]{:S(2)}, u32[]{:S(2)}) collective-permute-start(bf16[1024,128]{1,0:T(8,128)(2,1)S(1)} %collective-permute-done.2.rest), channel_id=1, source_target_pairs={{0,1},{1,2},{2,3},{4,5},{5,6},{6,7},{8,9},{9,10},{10,11},{12,13},{... | collective-permute-start | bytes 786440 | tf_op jit(solution)/shard_map/ppermute | solution.py:29
